TPU v7x, 32 devices: a whole 2x2x4 slice. The times are simulated.
32 devices in a mesh: row: 4 (over x, core), col: 8 (over z, y).
Axes of the slice: x: 2, y: 2, z: 4, core: 2. Of those that a mesh axis runs over, the one named last changes fastest.
Arguments:
- basis: bfloat16 [2, 8, 1536, 384], P(None, 'col', 'row'), may hold values from -0.078125 to 0.078125
- offsets: bfloat16 [2, 8, 3, 1536], P(None, 'col', None, 'row'), may hold values from -1 to 1
- centers: float32 [16, 3], replicated, may hold values from -1 to 16
- patch_points: int32 [16], replicated, may hold values from 768 to 1536, as said below
- base: float32 [4, 4, 128, 2, 8, 128], P(None, 'row', None, None, 'col'), may hold values from -1 to 33
Outputs:
- factored: float32 [4, 4, 128, 2, 8, 128], P(None, 'row', None, None, 'col')
Inputs may be any that keep to these rules, and one draw needn't show every extreme that they name: `patch_points`: every patch has at least 768 live points, and some patch has exactly 1536.
All inputs are finite; a program needn't handle non-finite values.
Results may differ from a plain program's by a relative error of at most 0.00066.
Values may be sent and summed in bfloat16 or wider, within the bound.
A program may use at most 64 MiB of HBM per device.

v0:
```python
import math

import jax
import jax.numpy as jnp
import numpy as np
from jax import lax
from jax.experimental import pallas as pl
from jax.experimental.pallas import tpu as pltpu
from jax.sharding import PartitionSpec as P

NB = 128
NCOMP = 3
NMAX = 1536
NPATCH = 16
PANEL = 128
NPANEL = 2


wave_number = 12.0
core_radius = 0.05
highest = lax.Precision.HIGHEST


cosine_series = (0.9999999890590201, -19.739204499453688, 64.93911745988827, -85.45013953077586, 60.16763095018129, -25.96759924584206, 6.528658157862129)
row_tile = 256
col_tile = 256


def pair_kernel(
    row_counts, col_counts, row_points_ref, col_points_ref, test_ref, basis_ref, out_ref, image_ref
):
    member, source, tile = pl.program_id(0), pl.program_id(1), pl.program_id(2)

    @pl.when(tile == 0)
    def _():
        out_ref[...] = jnp.zeros_like(out_ref)

    @pl.when(tile * row_tile < row_counts[member])
    def _():
        image_ref[...] = jnp.zeros_like(image_ref)
        row_points = row_points_ref[0]

        def one_chunk(chunk, carry):
            span = pl.ds(pl.multiple_of(chunk * col_tile, col_tile), col_tile)
            squared = jnp.zeros((row_tile, col_tile), jnp.float32)
            for axis in range(3):
                spacing = row_points[:, axis : axis + 1] - col_points_ref[0, axis : axis + 1, span]
                squared = squared + spacing * spacing
            distance = squared * lax.rsqrt(jnp.maximum(squared, 1e-30))
            turns = distance * (wave_number / (2.0 * math.pi))
            turns = turns - jnp.round(turns)
            square = turns * turns
            cosine = jnp.full_like(square, cosine_series[-1])
            for coefficient in cosine_series[-2::-1]:
                cosine = cosine * square + coefficient
            value = cosine * lax.rsqrt(squared + core_radius * core_radius)
            image_ref[...] += jnp.dot(
                value.astype(jnp.bfloat16), basis_ref[0, span, :], preferred_element_type=jnp.float32
            )
            return carry

        lax.fori_loop(0, (col_counts[source] + col_tile - 1) // col_tile, one_chunk, 0)
        image = image_ref[...].astype(jnp.bfloat16)
        total = out_ref[0, 0]
        for part in range(NCOMP):
            piece = slice(part * NB, (part + 1) * NB)
            total = total + lax.dot_general(
                test_ref[0, :, piece],
                image[:, piece],
                (((0,), (0,)), ((), ())),
                preferred_element_type=jnp.float32,
            )
        out_ref[0, 0] = total


def pair_blocks(row_counts, col_counts, row_points, col_points, tests, bases):
    members, sources, width = tests.shape[0], bases.shape[0], tests.shape[2]
    grid_spec = pltpu.PrefetchScalarGridSpec(
        num_scalar_prefetch=2,
        grid=(members, sources, NMAX // row_tile),
        in_specs=[
            pl.BlockSpec((1, row_tile, 3), lambda m, s, t, *_: (m, t, 0)),
            pl.BlockSpec((1, 3, NMAX), lambda m, s, t, *_: (s, 0, 0)),
            pl.BlockSpec((1, row_tile, width), lambda m, s, t, *_: (m, t, 0)),
            pl.BlockSpec((1, NMAX, width), lambda m, s, t, *_: (s, 0, 0)),
        ],
        out_specs=pl.BlockSpec((1, 1, NB, NB), lambda m, s, t, *_: (m, s, 0, 0)),
        scratch_shapes=[pltpu.VMEM((row_tile, width), jnp.float32)],
    )
    return pl.pallas_call(
        pair_kernel,
        out_shape=jax.ShapeDtypeStruct((members, sources, NB, NB), jnp.float32),
        grid_spec=grid_spec,
        compiler_params=pltpu.CompilerParams(vmem_limit_bytes=32 * 1024 * 1024),
    )(row_counts, col_counts, row_points, col_points, tests, bases)


def from_owner(value, axis, owner):
    count = lax.axis_size(axis)
    place = (lax.axis_index(axis) - owner) % count
    reach = 1
    while reach < count:
        steps = [
            ((owner + n) % count, (owner + n + reach) % count)
            for n in range(min(reach, count - reach))
        ]
        arrived = lax.ppermute(value, axis, steps)
        value = jnp.where(place < reach, value, arrived)
        reach *= 2
    return value


def panel_kernel(block_ref, factor_ref, lower_ref, upper_ref):
    order = block_ref.shape[0]
    rows = lax.broadcasted_iota(jnp.int32, (order, order), 0)
    cols = lax.broadcasted_iota(jnp.int32, (order, order), 1)
    row_ids = lax.broadcasted_iota(jnp.int32, (order, 1), 0)
    lanes = lax.broadcasted_iota(jnp.int32, (1, order), 1)
    identity = jnp.where(rows == cols, 1.0, 0.0).astype(jnp.float32)
    factor_ref[...] = block_ref[...]
    lower_ref[...] = identity
    upper_ref[...] = identity

    def one_column(k, carry):
        current = factor_ref[...]
        row = factor_ref[pl.ds(k, 1), :]
        lower_row = lower_ref[pl.ds(k, 1), :]
        upper = upper_ref[...]
        at_column = cols == k
        pivot = jnp.sum(jnp.where(lanes == k, row, 0.0), axis=1, keepdims=True)
        column = jnp.sum(jnp.where(at_column, current, 0.0), axis=1, keepdims=True)
        upper_column = jnp.sum(jnp.where(at_column, upper, 0.0), axis=1, keepdims=True)
        multiplier = jnp.where(row_ids > k, column / pivot, 0.0)
        right = jnp.where(lanes > k, row, 0.0)
        factor_ref[...] = jnp.where(
            jnp.logical_and(at_column, rows > k), multiplier, current - multiplier * right
        )
        lower_ref[...] = lower_ref[...] - multiplier * lower_row
        upper_ref[...] = jnp.where(
            at_column, upper_column / pivot, upper - upper_column * (right / pivot)
        )
        return carry

    lax.fori_loop(0, order, one_column, 0)


def factor_panel(block):
    shape = jax.ShapeDtypeStruct(block.shape, jnp.float32)
    spec = pl.BlockSpec(memory_space=pltpu.VMEM)
    return pl.pallas_call(
        panel_kernel,
        out_shape=[shape] * 3,
        in_specs=[spec],
        out_specs=[spec] * 3,
        compiler_params=pltpu.CompilerParams(vmem_limit_bytes=16 * 1024 * 1024),
    )(block)


def local(basis, offsets, centers, patch_points, base):
    row_count = lax.axis_size("row")
    col_count = lax.axis_size("col")
    row_index = lax.axis_index("row")
    col_index = lax.axis_index("col")
    col_blocks = basis.shape[0]
    slice_len = basis.shape[2]
    width = basis.shape[3]
    row_blocks = NPATCH // row_count
    whole_cols, whole_offsets = (
        lax.all_gather(basis, "row", axis=2, tiled=True),
        lax.all_gather(offsets, "row", axis=3, tiled=True),
    )
    source_centers = lax.dynamic_index_in_dim(
        centers.reshape(col_blocks, col_count, 3), col_index, 1, keepdims=False
    )
    source_counts = lax.dynamic_index_in_dim(
        patch_points.reshape(col_blocks, col_count), col_index, 1, keepdims=False
    )
    source_points = source_centers[:, :, None] + whole_offsets[:, 0].astype(jnp.float32)
    source_live = jnp.arange(NMAX)[None, :] < source_counts[:, None]
    source_basis = jnp.where(source_live[:, :, None], whole_cols[:, 0], 0)
    sliced, sliced_offsets = (
        lax.all_gather(basis, "col", axis=1, tiled=True),
        lax.all_gather(offsets, "col", axis=1, tiled=True),
    )
    all_slices = sliced.reshape(NPATCH, slice_len, width)
    all_offsets = sliced_offsets.reshape(NPATCH, 3, slice_len)
    class_sizes = patch_points.reshape(row_blocks, row_count)
    class_order = jnp.argsort(-class_sizes, axis=0, stable=True)
    members = jnp.stack(
        [
            jnp.stack(
                [
                    class_order[member, (group - member) % row_count] * row_count
                    + (group - member) % row_count
                    for member in range(row_blocks)
                ]
            )
            for group in range(row_count)
        ]
    )
    flat_members = members.reshape(-1)
    turned_offsets = jnp.transpose(all_offsets, (0, 2, 1))

    def picked(array, ids):
        return jnp.stack(
            [lax.dynamic_index_in_dim(array, ids[n], 0, keepdims=False) for n in range(ids.shape[0])]
        )

    send_basis = picked(all_slices, flat_members)
    send_offsets = picked(turned_offsets, flat_members)
    got_basis, got_offsets = (
        lax.all_to_all(send_basis, "row", split_axis=0, concat_axis=1, tiled=True),
        lax.all_to_all(send_offsets, "row", split_axis=0, concat_axis=1, tiled=True),
    )
    mine = lax.dynamic_index_in_dim(members, row_index, 0, keepdims=False)
    my_counts = jnp.stack(
        [lax.dynamic_index_in_dim(patch_points, mine[n], 0, False) for n in range(row_blocks)]
    )
    member_points = picked(centers, mine)[:, None, :] + got_offsets.astype(jnp.float32)
    member_live = jnp.arange(NMAX)[None, :] < my_counts[:, None]
    tests = jnp.where(member_live[:, :, None], got_basis, 0)
    stacked = pair_blocks(
        my_counts, source_counts, member_points, source_points, tests, source_basis
    ).transpose(0, 2, 1, 3)
    slot_count = (row_blocks + row_count - 1) // row_count
    slot_ids = (np.arange(slot_count) * row_count)[None, :].astype(np.int32)
    peer_ids = jnp.arange(row_count, dtype=jnp.int32)[:, None]
    send_member = slot_ids + (row_index - peer_ids) % row_count
    send_valid = send_member < row_blocks
    outgoing = jnp.where(
        send_valid[:, :, None, None, None], picked(stacked, jnp.minimum(send_member, row_blocks - 1).reshape(-1)).reshape(
            send_member.shape + stacked.shape[1:]
        ), 0.0
    )
    incoming = lax.all_to_all(outgoing, "row", split_axis=0, concat_axis=0, tiled=True)
    recv_member = slot_ids + (peer_ids - row_index) % row_count
    recv_valid = recv_member < row_blocks
    my_order = lax.dynamic_index_in_dim(class_order, row_index, 1, keepdims=False)
    recv_block = jnp.sum(
        jnp.where(
            jnp.minimum(recv_member, row_blocks - 1)[:, :, None] == jnp.arange(row_blocks),
            my_order,
            0,
        ),
        axis=2,
    )
    landing = jnp.logical_and(
        recv_valid[None], recv_block[None] == jnp.arange(row_blocks)[:, None, None]
    ).astype(jnp.float32)
    reduced = jnp.einsum("agt,gtuqv->auqv", landing, incoming, precision=highest).reshape(
        row_blocks, 1, NB, col_blocks, NB
    )
    matrix = (base + reduced.reshape(row_blocks, 1, NB, col_blocks, 1, NB)).reshape(
        row_blocks * NB, col_blocks * NB
    )
    row_global = (
        (jnp.arange(row_blocks)[:, None] * row_count + row_index) * NB + jnp.arange(NB)[None, :]
    ).reshape(-1)
    col_global = (
        (jnp.arange(col_blocks)[:, None] * col_count + col_index) * NB + jnp.arange(NB)[None, :]
    ).reshape(-1)
    for panel_index in range(NPANEL):
        start = panel_index * PANEL
        finish = start + PANEL
        panel_span = start + jnp.arange(PANEL)
        pick_cols = (col_global[:, None] == panel_span[None, :]).astype(jnp.float32)
        pick_rows = (panel_span[:, None] == row_global[None, :]).astype(jnp.float32)
        col_part = jnp.dot(matrix, pick_cols, precision=highest)
        col_panel = from_owner(col_part, "col", panel_index % col_count)
        diagonal_part = jnp.dot(pick_rows, col_panel, precision=highest)
        row_part = jnp.dot(pick_rows, matrix, precision=highest)
        joined = jnp.concatenate([diagonal_part, row_part], axis=1)
        joined = from_owner(joined, "row", panel_index % row_count)
        diagonal_block, row_panel = joined[:, :PANEL], joined[:, PANEL:]
        factored_block, lower_inverse, upper_inverse = factor_panel(diagonal_block)
        left = jnp.dot(col_panel, upper_inverse, precision=highest)
        right = jnp.dot(lower_inverse, row_panel, precision=highest)
        left_kept = jnp.where((row_global >= finish)[:, None], left, 0.0)
        right_kept = jnp.where((col_global >= finish)[None, :], right, 0.0)
        matrix = matrix - jnp.dot(left_kept, right_kept, precision=highest)
        diagonal_rows = jnp.dot(pick_rows.T, factored_block, precision=highest)
        new_columns = jnp.where(
            (row_global < start)[:, None],
            col_panel,
            jnp.where((row_global < finish)[:, None], diagonal_rows, left),
        )
        in_columns = jnp.logical_and(col_global >= start, col_global < finish)
        matrix = jnp.where(
            in_columns[None, :], jnp.dot(new_columns, pick_cols.T, precision=highest), matrix
        )
        in_rows = jnp.logical_and(row_global >= start, row_global < finish)
        upper_rows = jnp.dot(pick_rows.T, right, precision=highest)
        matrix = jnp.where(
            jnp.logical_and(in_rows[:, None], (col_global >= finish)[None, :]), upper_rows, matrix
        )
    return matrix.reshape(row_blocks, 1, NB, col_blocks, 1, NB)


def solution(mesh):
    in_specs = (
        P(None, "col", "row", None),
        P(None, "col", None, "row"),
        P(),
        P(),
        P(None, "row", None, None, "col", None),
    )
    out_specs = P(None, "row", None, None, "col", None)
    return jax.shard_map(local, mesh=mesh, in_specs=in_specs, out_specs=out_specs, check_vma=False)
```

profile of v0, /device:TPU:0, one launch (start us, length us, event | category | flops | bytes accessed | tf_op | source)
XLA Modules:
  0.0 468.6 jit_solution(13232074351391847248)
XLA Ops:
  40.6 33.3 %all_gather.12 = bf16[2,8,3,384]{3,0,2,1:T(2,128)(2,1)S(1)} all-gather(bf16[2,1,3,384]{3,0,2,1:T(2,128)(2,1)} %param.7), channel_id=1, replica_groups=mesh['row'=4,'col'=8] {'col'}, dimensions={1}, use_global_device_ids=true | all-gather | bytes 41472 | tf_op jit(solution)/shard_map/all_gather | solution.py:183
  85.0 3.3 all-to-all-start
  97.8 1.9 dynamic-slice_dynamic-update-slice_fusion.15
  99.7 1.8 dynamic-slice_dynamic-update-slice_fusion.14
  110.0 1.7 dynamic-slice_dynamic-update-slice_fusion.8
  117.8 5.1 %all-to-all-start.1 = ((bf16[16,384,384]{2,1,0:T(8,128)(2,1)}), bf16[16,384,384]{2,1,0:T(8,128)(2,1)}, u32[]{:S(2)}, u32[]{:S(2)}) async-start(bf16[16,384,384]{2,1,0:T(8,128)(2,1)} %dynamic-slice_dynamic-update-slice_fusion), calls=%async_computation.1 | async-start | bytes 9437184 | tf_op jit(solution)/shard_map/all_to_all | solution.py:212
  132.0 45.7 %all_gather.13 = bf16[2,1,3,1536]{3,2,0,1:T(4,128)(2,1)S(1)} all-gather(bf16[2,1,3,384]{3,2,0,1:T(4,128)(2,1)S(1)} %copy.78), channel_id=1, replica_groups=mesh['row'=4,'col'=8] {'row'}, dimensions={3}, use_global_device_ids=true | all-gather | bytes 23040 | tf_op jit(solution)/shard_map/all_gather | solution.py:170
  177.7 2.7 pad_add_fusion.1.row_counts
  180.7 2.3 copy.76
  183.0 2.1 bitcast_add_fusion.row_points_ref
  185.1 3.0 bitcast_select_fusion.1.basis_ref
  188.1 2.9 copy.79
  192.7 108.5 %shard_map.64 = f32[4,2,128,128]{3,2,1,0:T(8,128)S(1)} custom-call(s32[4]{0:T(128)S(1)} %pad_add_fusion.1.row_counts, s32[2]{0:T(128)S(1)} %fusion.87.col_counts, f32[4,1536,3]{2,1,0:T(8,128)S(1)} %bitcast_add_fusion.row_points_ref, f32[2,3,1536]{2,1,0:T(4,128)S(1)} %convert_add_fusion.col_points_ref, bf16[4,1536,384]{2,1,0:T(8,128)(2,1)S(1)} %bitcast_select_fusion.test_ref, ...), custom_call_target="tpu_custom_call" | custom-call | tf_op jit(solution)/shard_map/pallas_call | solution.py:90
  302.2 3.5 all-to-all-start.2
  306.2 8.4 %all-to-all-done.2 = f32[4,1,128,2,128]{4,2,3,1,0:T(8,128)S(1)} async-done(((f32[4,1,128,2,128]{4,2,3,1,0:T(8,128)}), f32[4,1,128,2,128]{4,2,3,1,0:T(8,128)S(1)}, u32[]{:S(2)}, u32[]{:S(2)}) %all-to-all-start.2) | async-done | bytes 524320 | tf_op jit(solution)/shard_map/all_to_all | solution.py:235
  317.4 34.6 %collective-permute-start = (f32[512,128]{1,0:T(8,128)S(1)}, f32[512,128]{1,0:T(8,128)S(1)}, u32[]{:S(2)}, u32[]{:S(2)}) collective-permute-start(f32[512,128]{1,0:T(8,128)S(1)} %fusion.6), channel_id=1, source_target_pairs={{0,1},{8,9},{16,17},{24,25}} | collective-permute-start | bytes 786440 | tf_op jit(solution)/shard_map/ppermute | solution.py:107
  352.0 5.3 %collective-permute-done = f32[512,128]{1,0:T(8,128)S(1)} collective-permute-done((f32[512,128]{1,0:T(8,128)S(1)}, f32[512,128]{1,0:T(8,128)S(1)}, u32[]{:S(2)}, u32[]{:S(2)}) %collective-permute-start) | collective-permute-done | bytes 262176 | tf_op jit(solution)/shard_map/ppermute | solution.py:107
  358.8 4.8 %collective-permute-done.1 = f32[512,128]{1,0:T(8,128)S(1)} collective-permute-done((f32[512,128]{1,0:T(8,128)S(1)}, f32[512,128]{1,0:T(8,128)S(1)}, u32[]{:S(2)}, u32[]{:S(2)}) %collective-permute-start.1) | collective-permute-done | bytes 262176 | tf_op jit(solution)/shard_map/ppermute | solution.py:107
  365.3 3.8 collective-permute-done.2
  373.3 4.8 %collective-permute-done.4 = f32[128,384]{1,0:T(8,128)S(1)} collective-permute-done((f32[128,384]{1,0:T(8,128)S(1)}, f32[128,384]{1,0:T(8,128)S(1)}, u32[]{:S(2)}, u32[]{:S(2)}) %collective-permute-start.4) | collective-permute-done | bytes 196640 | tf_op jit(solution)/shard_map/ppermute | solution.py:107
  378.1 14.6 %shard_map.65 = (f32[128,128]{1,0:T(8,128)S(1)}, f32[128,128]{1,0:T(8,128)S(1)}, f32[128,128]{1,0:T(8,128)S(1)}) custom-call(f32[128,128]{1,0:T(8,128)S(1)} %slice.204.block_ref), custom_call_target="tpu_custom_call" | custom-call | tf_op jit(solution)/shard_map/pallas_call | solution.py:150
  399.1 29.3 %collective-permute-done.7 = f32[512,128]{1,0:T(8,128)S(1)} collective-permute-done((f32[512,128]{1,0:T(8,128)S(1)}, f32[512,128]{1,0:T(8,128)S(1)}, u32[]{:S(2)}, u32[]{:S(2)}) %collective-permute-start.7) | collective-permute-done | bytes 262176 | tf_op jit(solution)/shard_map/ppermute | solution.py:107
  430.9 12.4 %collective-permute-done.9 = f32[128,384]{1,0:T(8,128)S(1)} collective-permute-done((f32[128,384]{1,0:T(8,128)S(1)}, f32[128,384]{1,0:T(8,128)S(1)}, u32[]{:S(2)}, u32[]{:S(2)}) %collective-permute-start.9) | collective-permute-done | bytes 196640 | tf_op jit(solution)/shard_map/ppermute | solution.py:107
  443.3 14.6 %shard_map.66 = (f32[128,128]{1,0:T(8,128)S(1)}, f32[128,128]{1,0:T(8,128)S(1)}, f32[128,128]{1,0:T(8,128)S(1)}) custom-call(f32[128,128]{1,0:T(8,128)S(1)} %slice.206.block_ref), custom_call_target="tpu_custom_call" | custom-call | tf_op jit(solution)/shard_map/pallas_call | solution.py:150
  (128 shorter events, 48.8 us)
Async XLA Ops:
  6.5 91.3 %all-gather.3.cloned.1.call-start = ((), (), s32[]{:S(2)}) async-start(), calls=%async_computation.3 | async-start | bytes 5308416 | tf_op jit(solution)/shard_map/all_gather | solution.py:182
  85.0 32.8 %all-to-all-start = ((bf16[16,384,3]{1,2,0:T(4,128)(2,1)}), bf16[16,384,3]{1,2,0:T(4,128)(2,1)S(1)}, u32[]{:S(2)}, u32[]{:S(2)}) async-start(bf16[16,384,3]{1,2,0:T(4,128)(2,1)} %copy.74), calls=%async_computation | async-start | bytes 98304 | tf_op jit(solution)/shard_map/all_to_all | solution.py:213
  88.3 96.9 %all-gather.5.cloned.1.call-start = ((), (), s32[]{:S(2)}) async-start(), calls=%async_computation.4 | async-start | bytes 2949120 | tf_op jit(solution)/shard_map/all_gather | solution.py:169
  97.8 14.0 %copy-start.1 = (bf16[2,8,384,384]{3,2,1,0:T(8,128)(2,1)S(1)}, bf16[2,8,384,384]{3,2,1,0:T(8,128)(2,1)}, u32[]{:S(2)}) copy-start(bf16[2,8,384,384]{3,2,1,0:T(8,128)(2,1)} %all-gather.3.cloned.1.call-done) | copy-start | bytes 14155780
  117.8 5.1 %copy-start.2 = (f32[16,3]{0,1:T(4,128)S(1)}, f32[16,3]{0,1:T(4,128)}, u32[]{:S(2)}) copy-start(f32[16,3]{0,1:T(4,128)} %param.8) | copy-start | bytes 580
  117.8 5.2 %copy-start.4 = (s32[16]{0:T(128)S(1)}, s32[16]{0:T(128)}, u32[]{:S(2)}) copy-start(s32[16]{0:T(128)} %param.9) | copy-start | bytes 196
  117.8 5.4 %copy-start.3 = (bf16[2,1,3,384]{3,0,2,1:T(2,128)(2,1)S(1)}, bf16[2,1,3,384]{3,0,2,1:T(2,128)(2,1)}, u32[]{:S(2)}) copy-start(bf16[2,1,3,384]{3,0,2,1:T(2,128)(2,1)} %param.7) | copy-start | bytes 13828
  117.8 70.3 %all-to-all-start.1 = ((bf16[16,384,384]{2,1,0:T(8,128)(2,1)}), bf16[16,384,384]{2,1,0:T(8,128)(2,1)}, u32[]{:S(2)}, u32[]{:S(2)}) async-start(bf16[16,384,384]{2,1,0:T(8,128)(2,1)} %dynamic-slice_dynamic-update-slice_fusion), calls=%async_computation.1 | async-start | bytes 9437184 | tf_op jit(solution)/shard_map/all_to_all | solution.py:212
  191.1 1.7 copy-start
  302.2 12.3 %all-to-all-start.2 = ((f32[4,1,128,2,128]{4,2,3,1,0:T(8,128)}), f32[4,1,128,2,128]{4,2,3,1,0:T(8,128)S(1)}, u32[]{:S(2)}, u32[]{:S(2)}) async-start(f32[4,1,128,2,128]{4,2,3,1,0:T(8,128)} %maximum_select_fusion), calls=%async_computation.2 | async-start | bytes 1048576 | tf_op jit(solution)/shard_map/all_to_all | solution.py:235
  317.4 39.9 %collective-permute-start = (f32[512,128]{1,0:T(8,128)S(1)}, f32[512,128]{1,0:T(8,128)S(1)}, u32[]{:S(2)}, u32[]{:S(2)}) collective-permute-start(f32[512,128]{1,0:T(8,128)S(1)} %fusion.6), channel_id=1, source_target_pairs={{0,1},{8,9},{16,17},{24,25}} | collective-permute-start | bytes 786440 | tf_op jit(solution)/shard_map/ppermute | solution.py:107
  357.4 6.2 %collective-permute-start.1 = (f32[512,128]{1,0:T(8,128)S(1)}, f32[512,128]{1,0:T(8,128)S(1)}, u32[]{:S(2)}, u32[]{:S(2)}) collective-permute-start(f32[512,128]{1,0:T(8,128)S(1)} %broadcast_select_fusion), channel_id=1, source_target_pairs={{0,2},{1,3},{8,10},{9,11},{16,18},{17,19},{24,26},{25,27}} | collective-permute-start | bytes 786440 | tf_op jit(solution)/shard_map/ppermute | solution.py:107
  363.6 5.5 %collective-permute-start.2 = (f32[512,128]{1,0:T(8,128)S(1)}, f32[512,128]{1,0:T(8,128)S(1)}, u32[]{:S(2)}, u32[]{:S(2)}) collective-permute-start(f32[512,128]{1,0:T(8,128)S(1)} %broadcast_select_fusion.1), channel_id=1, source_target_pairs={{0,4},{1,5},{2,6},{3,7},{8,12},{9,13},{10,14},{11,15},{16,20},{17,... | collective-permute-start | bytes 786440 | tf_op jit(solution)/shard_map/ppermute | solution.py:107
  369.4 2.4 collective-permute-start.3
  371.8 6.3 %collective-permute-start.4 = (f32[128,384]{1,0:T(8,128)S(1)}, f32[128,384]{1,0:T(8,128)S(1)}, u32[]{:S(2)}, u32[]{:S(2)}) collective-permute-start(f32[128,384]{1,0:T(8,128)S(1)} %broadcast_select_fusion.6), channel_id=1, source_target_pairs={{0,16},{8,24},{1,17},{9,25},{2,18},{10,26},{3,19},{11,27},{4,20},{... | collective-permute-start | bytes 589832 | tf_op jit(solution)/shard_map/ppermute | solution.py:107
  395.8 0.7 collective-permute-start.5
  396.6 0.9 collective-permute-start.6
  397.5 31.0 %collective-permute-start.7 = (f32[512,128]{1,0:T(8,128)S(1)}, f32[512,128]{1,0:T(8,128)S(1)}, u32[]{:S(2)}, u32[]{:S(2)}) collective-permute-start(f32[512,128]{1,0:T(8,128)S(1)} %broadcast_select_fusion.4), channel_id=1, source_target_pairs={{1,5},{2,6},{3,7},{4,0},{9,13},{10,14},{11,15},{12,8},{17,21},{18,... | collective-permute-start | bytes 786440 | tf_op jit(solution)/shard_map/ppermute | solution.py:107
  428.8 0.7 collective-permute-start.8
  429.6 13.7 %collective-permute-start.9 = (f32[128,384]{1,0:T(8,128)S(1)}, f32[128,384]{1,0:T(8,128)S(1)}, u32[]{:S(2)}, u32[]{:S(2)}) collective-permute-start(f32[128,384]{1,0:T(8,128)S(1)} %broadcast_select_fusion.8), channel_id=1, source_target_pairs={{8,24},{16,0},{9,25},{17,1},{10,26},{18,2},{11,27},{19,3},{12,28},... | collective-permute-start | bytes 589832 | tf_op jit(solution)/shard_map/ppermute | solution.py:107
Sparse Core Ops, SparseCore 0:
  9.5 83.1 all-gather.2
  94.3 22.2 all-gather.4
where the time goes:
time: 461 us; the launch traced here: 469 us
  Pallas kernels  138 us (30%)
  blocking collectives  79 us (17%)
  waiting for transfers between devices  71.1 us (15%)
  between operations  69.6 us (15%)
  starting transfers between devices  56.5 us (12%)
  local copies, waits for them, and re-layouts  32.7 us (7%)
  other arithmetic  13.6 us (3%)
  matrix products  8.39 us (2%)
    pallas_call x1, Pallas kernels, pair_blocks(): pl.pallas_call(pair_kernel, out_shape=jax.ShapeDtypeStruct((members, sour...  109 us
    ppermute x10, waiting for transfers between devices, from_owner(): arrived = lax.ppermute(value, axis, steps)  61.3 us
    all_gather x1, blocking collectives, local(): lax.all_gather(offsets, 'row', axis=3, tiled=True)  45.7 us
    ppermute x10, starting transfers between devices, from_owner(): arrived = lax.ppermute(value, axis, steps)  44.7 us
    all_gather x1, blocking collectives, local(): lax.all_gather(offsets, 'col', axis=1, tiled=True)  33.3 us
    pallas_call x2, Pallas kernels, factor_panel(): pl.pallas_call(panel_kernel, out_shape=[shape] * 3, in_specs=[spec], out_...  29.3 us
    unnamed x26, local copies, waits for them, and re-layouts  19.7 us
  transfers between devices with their start and end apart: 15, of which 8 were waited for; matrix products, arithmetic and copies ran while one was open for 8% of the time, Pallas kernels for 0%

commit v1 on v0

--- a/solution.py
+++ b/solution.py
@@ -95,6 +95,23 @@
     )(row_counts, col_counts, row_points, col_points, tests, bases)
 
 
+def gather_direct(value, axis, dim):
+    count, here, size = lax.axis_size(axis), lax.axis_index(axis), value.shape[dim]
+    shape = list(value.shape)
+    shape[dim] = size * count
+    whole = lax.dynamic_update_slice_in_dim(
+        jnp.zeros(shape, value.dtype), value, here * size, dim
+    )
+    arrivals = [
+        lax.ppermute(value, axis, [(n, (n + shift) % count) for n in range(count)])
+        for shift in range(1, count)
+    ]
+    for shift, arrived in enumerate(arrivals, 1):
+        place = (here - shift) % count
+        whole = lax.dynamic_update_slice_in_dim(whole, arrived, place * size, dim)
+    return whole
+
+
 def from_owner(value, axis, owner):
     count = lax.axis_size(axis)
     place = (lax.axis_index(axis) - owner) % count
@@ -166,8 +183,8 @@
     width = basis.shape[3]
     row_blocks = NPATCH // row_count
     whole_cols, whole_offsets = (
-        lax.all_gather(basis, "row", axis=2, tiled=True),
-        lax.all_gather(offsets, "row", axis=3, tiled=True),
+        gather_direct(basis, "row", 2),
+        gather_direct(offsets, "row", 3),
     )
     source_centers = lax.dynamic_index_in_dim(
         centers.reshape(col_blocks, col_count, 3), col_index, 1, keepdims=False

time: 461 us -> 467 us (1.013); the launches traced: 469 us -> 459 us
  blocking collectives: 79 us -> 31.9 us
  waiting for transfers between devices: 71.1 us -> 114 us
  Pallas kernels: 138 us -> 113 us
  local copies, waits for them, and re-layouts: 32.7 us -> 46.4 us
  starting transfers between devices: 56.5 us -> 62.9 us
    all_gather x1 -> x0, blocking collectives: 45.7 us -> none  [local(): lax.all_gather(offsets, 'row', axis=3, tiled=True)]
    ppermute x0 -> x6, waiting for transfers between devices: none -> 42 us  [gather_direct(): lax.ppermute(value, axis, [(n, (n + shift) % count) for n in range(count)])]
    pallas_call x1, Pallas kernels: 109 us -> 83.7 us  [pair_blocks(): pl.pallas_call(pair_kernel, out_shape=jax.ShapeDtypeStruct((members, sour...]
    dynamic_update_slice x0 -> x8, local copies, waits for them, and re-layouts: none -> 8.54 us  [the longest x6 5.88 us: gather_direct(): whole = lax.dynamic_update_slice_in_dim(whole, arrived, place * size, dim)]
    ppermute x0 -> x6, starting transfers between devices: none -> 6.63 us  [gather_direct(): lax.ppermute(value, axis, [(n, (n + shift) % count) for n in range(count)])]
    unnamed x26 -> x20, local copies, waits for them, and re-layouts: 19.7 us -> 20.4 us
  transfers between devices with their start and end apart: 15 -> 20, of which waited for: 8 -> 9; matrix products, arithmetic and copies ran while one was open for 8% -> 11% of each run, Pallas kernels for 0% -> 0%
where the time goes in v1:
time: 467 us; the launch traced here: 459 us
  waiting for transfers between devices  114 us (24%)
  Pallas kernels  113 us (24%)
  between operations  69.8 us (15%)
  starting transfers between devices  62.9 us (13%)
  local copies, waits for them, and re-layouts  46.4 us (10%)
  blocking collectives  31.9 us (7%)
  other arithmetic  13.5 us (3%)
  matrix products  8.39 us (2%)
    pallas_call x1, Pallas kernels, pair_blocks(): pl.pallas_call(pair_kernel, out_shape=jax.ShapeDtypeStruct((members, sour...  83.7 us
    ppermute x10, waiting for transfers between devices, from_owner(): arrived = lax.ppermute(value, axis, steps)  62.5 us
    ppermute x10, starting transfers between devices, from_owner(): arrived = lax.ppermute(value, axis, steps)  44.6 us
    ppermute x6, waiting for transfers between devices, gather_direct(): lax.ppermute(value, axis, [(n, (n + shift) % count) for n in range(count)])  42 us
    all_gather x1, blocking collectives, local(): lax.all_gather(offsets, 'col', axis=1, tiled=True)  31.9 us
    pallas_call x2, Pallas kernels, factor_panel(): pl.pallas_call(panel_kernel, out_shape=[shape] * 3, in_specs=[spec], out_...  29.3 us
    unnamed x20, local copies, waits for them, and re-layouts  20.4 us
  transfers between devices with their start and end apart: 20, of which 9 were waited for; matrix products, arithmetic and copies ran while one was open for 11% of the time, Pallas kernels for 0%

profile of v1, /device:TPU:0, one launch (start us, length us, event | category | flops | bytes accessed | tf_op | source)
XLA Modules:
  0.0 459.5 jit_solution(10461446340746535176)
XLA Ops:
  7.8 2.6 collective-permute-start.4
  46.2 31.9 %all_gather.6 = bf16[2,8,3,384]{3,0,2,1:T(2,128)(2,1)S(1)} all-gather(bf16[2,1,3,384]{3,0,2,1:T(2,128)(2,1)} %param.7), channel_id=1, replica_groups=mesh['row'=4,'col'=8] {'col'}, dimensions={1}, use_global_device_ids=true | all-gather | bytes 41472 | tf_op jit(solution)/shard_map/all_gather | solution.py:200
  89.1 3.3 all-to-all-start
  103.9 2.6 pad_add_fusion.1.row_counts
  132.6 4.9 %all-to-all-start.1 = ((bf16[16,384,384]{2,1,0:T(8,128)(2,1)}), bf16[16,384,384]{2,1,0:T(8,128)(2,1)}, u32[]{:S(2)}, u32[]{:S(2)}) async-start(bf16[16,384,384]{2,1,0:T(8,128)(2,1)} %dynamic-slice_dynamic-update-slice_fusion), calls=%async_computation.1 | async-start | bytes 9437184 | tf_op jit(solution)/shard_map/all_to_all | solution.py:229
  147.3 42.0 %collective-permute-done.2 = bf16[2,1,3,384]{3,2,0,1:T(4,128)(2,1)S(1)} collective-permute-done((bf16[2,1,3,384]{3,2,0,1:T(4,128)(2,1)S(1)}, bf16[2,1,3,384]{3,2,0,1:T(4,128)(2,1)S(1)}, u32[]{:S(2)}, u32[]{:S(2)}) %collective-permute-start.2) | collective-permute-done | bytes 4640 | tf_op jit(solution)/shard_map/ppermute | solution.py:106
  189.4 2.3 copy.101
  191.8 2.1 bitcast_add_fusion.row_points_ref
  197.8 2.0 bitcast_dynamic-update-slice_fusion
  199.7 2.9 broadcast_select_fusion.basis_ref
  202.7 2.9 copy.107
  207.3 83.7 %shard_map.64 = f32[4,2,128,128]{3,2,1,0:T(8,128)S(1)} custom-call(s32[4]{0:T(128)S(1)} %pad_add_fusion.1.row_counts, s32[2]{0:T(128)S(1)} %fusion.87.col_counts, f32[4,1536,3]{2,1,0:T(8,128)S(1)} %bitcast_add_fusion.row_points_ref, f32[2,3,1536]{2,1,0:T(4,128)S(1)} %convert_add_fusion.col_points_ref, bf16[4,1536,384]{2,1,0:T(8,128)(2,1)S(1)} %bitcast_select_fusion.test_ref, ...), custom_call_target="tpu_custom_call" | custom-call | tf_op jit(solution)/shard_map/pallas_call | solution.py:90
  292.0 3.5 all-to-all-start.2
  295.9 8.4 %all-to-all-done.2 = f32[4,1,128,2,128]{4,2,3,1,0:T(8,128)S(1)} async-done(((f32[4,1,128,2,128]{4,2,3,1,0:T(8,128)}), f32[4,1,128,2,128]{4,2,3,1,0:T(8,128)S(1)}, u32[]{:S(2)}, u32[]{:S(2)}) %all-to-all-start.2) | async-done | bytes 524320 | tf_op jit(solution)/shard_map/all_to_all | solution.py:252
  307.2 33.0 %collective-permute-start.6 = (f32[512,128]{1,0:T(8,128)S(1)}, f32[512,128]{1,0:T(8,128)S(1)}, u32[]{:S(2)}, u32[]{:S(2)}) collective-permute-start(f32[512,128]{1,0:T(8,128)S(1)} %fusion.6), channel_id=1, source_target_pairs={{0,1},{8,9},{16,17},{24,25}} | collective-permute-start | bytes 786440 | tf_op jit(solution)/shard_map/ppermute | solution.py:124
  340.2 5.3 %collective-permute-done.6 = f32[512,128]{1,0:T(8,128)S(1)} collective-permute-done((f32[512,128]{1,0:T(8,128)S(1)}, f32[512,128]{1,0:T(8,128)S(1)}, u32[]{:S(2)}, u32[]{:S(2)}) %collective-permute-start.6) | collective-permute-done | bytes 262176 | tf_op jit(solution)/shard_map/ppermute | solution.py:124
  345.5 2.9 collective-permute-start.7
  348.5 5.2 %collective-permute-done.7 = f32[512,128]{1,0:T(8,128)S(1)} collective-permute-done((f32[512,128]{1,0:T(8,128)S(1)}, f32[512,128]{1,0:T(8,128)S(1)}, u32[]{:S(2)}, u32[]{:S(2)}) %collective-permute-start.7) | collective-permute-done | bytes 262176 | tf_op jit(solution)/shard_map/ppermute | solution.py:124
  355.5 4.4 collective-permute-done.8
  364.2 4.7 %collective-permute-done.10 = f32[128,384]{1,0:T(8,128)S(1)} collective-permute-done((f32[128,384]{1,0:T(8,128)S(1)}, f32[128,384]{1,0:T(8,128)S(1)}, u32[]{:S(2)}, u32[]{:S(2)}) %collective-permute-start.10) | collective-permute-done | bytes 196640 | tf_op jit(solution)/shard_map/ppermute | solution.py:124
  368.9 14.6 %shard_map.65 = (f32[128,128]{1,0:T(8,128)S(1)}, f32[128,128]{1,0:T(8,128)S(1)}, f32[128,128]{1,0:T(8,128)S(1)}) custom-call(f32[128,128]{1,0:T(8,128)S(1)} %slice.204.block_ref), custom_call_target="tpu_custom_call" | custom-call | tf_op jit(solution)/shard_map/pallas_call | solution.py:167
  389.8 29.5 %collective-permute-done.13 = f32[512,128]{1,0:T(8,128)S(1)} collective-permute-done((f32[512,128]{1,0:T(8,128)S(1)}, f32[512,128]{1,0:T(8,128)S(1)}, u32[]{:S(2)}, u32[]{:S(2)}) %collective-permute-start.13) | collective-permute-done | bytes 262176 | tf_op jit(solution)/shard_map/ppermute | solution.py:124
  421.7 12.4 %collective-permute-done.15 = f32[128,384]{1,0:T(8,128)S(1)} collective-permute-done((f32[128,384]{1,0:T(8,128)S(1)}, f32[128,384]{1,0:T(8,128)S(1)}, u32[]{:S(2)}, u32[]{:S(2)}) %collective-permute-start.15) | collective-permute-done | bytes 196640 | tf_op jit(solution)/shard_map/ppermute | solution.py:124
  434.1 14.6 %shard_map.66 = (f32[128,128]{1,0:T(8,128)S(1)}, f32[128,128]{1,0:T(8,128)S(1)}, f32[128,128]{1,0:T(8,128)S(1)}) custom-call(f32[128,128]{1,0:T(8,128)S(1)} %slice.206.block_ref), custom_call_target="tpu_custom_call" | custom-call | tf_op jit(solution)/shard_map/pallas_call | solution.py:167
  (140 shorter events, 67.8 us)
Async XLA Ops:
  6.5 106.1 %all-gather.2.cloned.1.call-start = ((), (), s32[]{:S(2)}) async-start(), calls=%async_computation.3 | async-start | bytes 5308416 | tf_op jit(solution)/shard_map/all_gather | solution.py:199
  7.3 186.6 %collective-permute-start.3 = (bf16[2,1,384,384]{3,2,0,1:T(8,128)(2,1)}, bf16[2,1,384,384]{3,2,0,1:T(8,128)(2,1)}, u32[]{:S(2)}, u32[]{:S(2)}) collective-permute-start(bf16[2,1,384,384]{3,2,0,1:T(8,128)(2,1)} %bitcast.217), channel_id=1, source_target_pairs={{0,8},{8,16},{16,24},{24,0},{1,9},{9,17},{17,25},{25,1},{2,10},{10... | collective-permute-start | bytes 1769480 | tf_op jit(solution)/shard_map/ppermute | solution.py:106
  7.8 188.1 %collective-permute-start.4 = (bf16[2,1,384,384]{3,2,0,1:T(8,128)(2,1)}, bf16[2,1,384,384]{3,2,0,1:T(8,128)(2,1)}, u32[]{:S(2)}, u32[]{:S(2)}) collective-permute-start(bf16[2,1,384,384]{3,2,0,1:T(8,128)(2,1)} %bitcast.218), channel_id=1, source_target_pairs={{0,16},{8,24},{16,0},{24,8},{1,17},{9,25},{17,1},{25,9},{2,18},{10... | collective-permute-start | bytes 1769480 | tf_op jit(solution)/shard_map/ppermute | solution.py:106
  10.3 187.4 %collective-permute-start.5 = (bf16[2,1,384,384]{3,2,0,1:T(8,128)(2,1)}, bf16[2,1,384,384]{3,2,0,1:T(8,128)(2,1)}, u32[]{:S(2)}, u32[]{:S(2)}) collective-permute-start(bf16[2,1,384,384]{3,2,0,1:T(8,128)(2,1)} %bitcast.219), channel_id=1, source_target_pairs={{0,24},{8,0},{16,8},{24,16},{1,25},{9,1},{17,9},{25,17},{2,26},{10... | collective-permute-start | bytes 1769480 | tf_op jit(solution)/shard_map/ppermute | solution.py:106
  12.4 133.1 %collective-permute-start = (bf16[2,1,3,384]{3,2,0,1:T(4,128)(2,1)S(1)}, bf16[2,1,3,384]{3,2,0,1:T(4,128)(2,1)S(1)}, u32[]{:S(2)}, u32[]{:S(2)}) collective-permute-start(bf16[2,1,3,384]{3,2,0,1:T(4,128)(2,1)S(1)} %copy.103), channel_id=1, source_target_pairs={{0,8},{8,16},{16,24},{24,0},{1,9},{9,17},{17,25},{25,1},{2,10},{10... | collective-permute-start | bytes 13832 | tf_op jit(solution)/shard_map/ppermute | solution.py:106
  12.4 134.8 %collective-permute-start.1 = (bf16[2,1,3,384]{3,2,0,1:T(4,128)(2,1)S(1)}, bf16[2,1,3,384]{3,2,0,1:T(4,128)(2,1)S(1)}, u32[]{:S(2)}, u32[]{:S(2)}) collective-permute-start(bf16[2,1,3,384]{3,2,0,1:T(4,128)(2,1)S(1)} %copy.103), channel_id=1, source_target_pairs={{0,16},{8,24},{16,0},{24,8},{1,17},{9,25},{17,1},{25,9},{2,18},{10... | collective-permute-start | bytes 13832 | tf_op jit(solution)/shard_map/ppermute | solution.py:106
  89.1 43.5 %all-to-all-start = ((bf16[16,384,3]{1,2,0:T(4,128)(2,1)}), bf16[16,384,3]{1,2,0:T(4,128)(2,1)S(1)}, u32[]{:S(2)}, u32[]{:S(2)}) async-start(bf16[16,384,3]{1,2,0:T(4,128)(2,1)} %copy.99), calls=%async_computation | async-start | bytes 98304 | tf_op jit(solution)/shard_map/all_to_all | solution.py:230
  112.7 13.9 %copy-start.1 = (bf16[2,8,384,384]{3,2,1,0:T(8,128)(2,1)S(1)}, bf16[2,8,384,384]{3,2,1,0:T(8,128)(2,1)}, u32[]{:S(2)}) copy-start(bf16[2,8,384,384]{3,2,1,0:T(8,128)(2,1)} %all-gather.2.cloned.1.call-done) | copy-start | bytes 14155780
  132.6 70.0 %all-to-all-start.1 = ((bf16[16,384,384]{2,1,0:T(8,128)(2,1)}), bf16[16,384,384]{2,1,0:T(8,128)(2,1)}, u32[]{:S(2)}, u32[]{:S(2)}) async-start(bf16[16,384,384]{2,1,0:T(8,128)(2,1)} %dynamic-slice_dynamic-update-slice_fusion), calls=%async_computation.1 | async-start | bytes 9437184 | tf_op jit(solution)/shard_map/all_to_all | solution.py:229
  145.5 43.8 %collective-permute-start.2 = (bf16[2,1,3,384]{3,2,0,1:T(4,128)(2,1)S(1)}, bf16[2,1,3,384]{3,2,0,1:T(4,128)(2,1)S(1)}, u32[]{:S(2)}, u32[]{:S(2)}) collective-permute-start(bf16[2,1,3,384]{3,2,0,1:T(4,128)(2,1)S(1)} %copy.103), channel_id=1, source_target_pairs={{0,24},{8,0},{16,8},{24,16},{1,25},{9,1},{17,9},{25,17},{2,26},{10... | collective-permute-start | bytes 13832 | tf_op jit(solution)/shard_map/ppermute | solution.py:106
  205.6 1.7 copy-start
  292.0 12.3 %all-to-all-start.2 = ((f32[4,1,128,2,128]{4,2,3,1,0:T(8,128)}), f32[4,1,128,2,128]{4,2,3,1,0:T(8,128)S(1)}, u32[]{:S(2)}, u32[]{:S(2)}) async-start(f32[4,1,128,2,128]{4,2,3,1,0:T(8,128)} %maximum_select_fusion), calls=%async_computation.2 | async-start | bytes 1048576 | tf_op jit(solution)/shard_map/all_to_all | solution.py:252
  307.2 38.3 %collective-permute-start.6 = (f32[512,128]{1,0:T(8,128)S(1)}, f32[512,128]{1,0:T(8,128)S(1)}, u32[]{:S(2)}, u32[]{:S(2)}) collective-permute-start(f32[512,128]{1,0:T(8,128)S(1)} %fusion.6), channel_id=1, source_target_pairs={{0,1},{8,9},{16,17},{24,25}} | collective-permute-start | bytes 786440 | tf_op jit(solution)/shard_map/ppermute | solution.py:124
  345.5 8.2 %collective-permute-start.7 = (f32[512,128]{1,0:T(8,128)S(1)}, f32[512,128]{1,0:T(8,128)S(1)}, u32[]{:S(2)}, u32[]{:S(2)}) collective-permute-start(f32[512,128]{1,0:T(8,128)S(1)} %broadcast_select_fusion.1), channel_id=1, source_target_pairs={{0,2},{1,3},{8,10},{9,11},{16,18},{17,19},{24,26},{25,27}} | collective-permute-start | bytes 786440 | tf_op jit(solution)/shard_map/ppermute | solution.py:124
  353.8 6.1 %collective-permute-start.8 = (f32[512,128]{1,0:T(8,128)S(1)}, f32[512,128]{1,0:T(8,128)S(1)}, u32[]{:S(2)}, u32[]{:S(2)}) collective-permute-start(f32[512,128]{1,0:T(8,128)S(1)} %broadcast_select_fusion.2), channel_id=1, source_target_pairs={{0,4},{1,5},{2,6},{3,7},{8,12},{9,13},{10,14},{11,15},{16,20},{17,... | collective-permute-start | bytes 786440 | tf_op jit(solution)/shard_map/ppermute | solution.py:124
  360.2 2.4 collective-permute-start.9
  362.6 6.3 %collective-permute-start.10 = (f32[128,384]{1,0:T(8,128)S(1)}, f32[128,384]{1,0:T(8,128)S(1)}, u32[]{:S(2)}, u32[]{:S(2)}) collective-permute-start(f32[128,384]{1,0:T(8,128)S(1)} %broadcast_select_fusion.7), channel_id=1, source_target_pairs={{0,16},{8,24},{1,17},{9,25},{2,18},{10,26},{3,19},{11,27},{4,20},{... | collective-permute-start | bytes 589832 | tf_op jit(solution)/shard_map/ppermute | solution.py:124
  386.6 0.7 collective-permute-start.11
  387.4 0.7 collective-permute-start.12
  388.1 31.2 %collective-permute-start.13 = (f32[512,128]{1,0:T(8,128)S(1)}, f32[512,128]{1,0:T(8,128)S(1)}, u32[]{:S(2)}, u32[]{:S(2)}) collective-permute-start(f32[512,128]{1,0:T(8,128)S(1)} %broadcast_select_fusion.5), channel_id=1, source_target_pairs={{1,5},{2,6},{3,7},{4,0},{9,13},{10,14},{11,15},{12,8},{17,21},{18,... | collective-permute-start | bytes 786440 | tf_op jit(solution)/shard_map/ppermute | solution.py:124
  419.7 0.7 collective-permute-start.14
  420.4 13.7 %collective-permute-start.15 = (f32[128,384]{1,0:T(8,128)S(1)}, f32[128,384]{1,0:T(8,128)S(1)}, u32[]{:S(2)}, u32[]{:S(2)}) collective-permute-start(f32[128,384]{1,0:T(8,128)S(1)} %broadcast_select_fusion.9), channel_id=1, source_target_pairs={{8,24},{16,0},{9,25},{17,1},{10,26},{18,2},{11,27},{19,3},{12,28},... | collective-permute-start | bytes 589832 | tf_op jit(solution)/shard_map/ppermute | solution.py:124
Sparse Core Ops, SparseCore 0:
  9.5 83.2 all-gather.1

commit v2 on v1

--- a/solution.py
+++ b/solution.py
@@ -199,6 +199,7 @@
         lax.all_gather(basis, "col", axis=1, tiled=True),
         lax.all_gather(offsets, "col", axis=1, tiled=True),
     )
+    sliced, whole_cols = lax.optimization_barrier((sliced, whole_cols))
     all_slices = sliced.reshape(NPATCH, slice_len, width)
     all_offsets = sliced_offsets.reshape(NPATCH, 3, slice_len)
     class_sizes = patch_points.reshape(row_blocks, row_count)

time: 467 us -> 471 us (level); the launches traced: 459 us -> 475 us
  Pallas kernels: 113 us -> 157 us
  starting transfers between devices: 62.9 us -> 41.4 us
    pallas_call x1, Pallas kernels: 83.7 us -> 127 us  [pair_blocks(): pl.pallas_call(pair_kernel, out_shape=jax.ShapeDtypeStruct((members, sour...]
    ppermute x6, waiting for transfers between devices: 42 us -> 0.02 us  [gather_direct(): lax.ppermute(value, axis, [(n, (n + shift) % count) for n in range(count)])]
    all_to_all x1, waiting for transfers between devices: 0.01 us -> 38.3 us  [local(): lax.all_to_all(send_basis, 'row', split_axis=0, concat_axis=1, tiled=True)]
    ppermute x10, starting transfers between devices: 44.6 us -> 13 us  [from_owner(): arrived = lax.ppermute(value, axis, steps)]
    all_to_all x1, starting transfers between devices: 3.47 us -> 13.7 us  [local(): lax.all_to_all(outgoing, 'row', split_axis=0, concat_axis=0, tiled=True)]
  transfers between devices with their start and end apart: 20 -> 20, of which waited for: 9 -> 9; matrix products, arithmetic and copies ran while one was open for 11% -> 10% of each run, Pallas kernels for 0% -> 0%
where the time goes in v2:
time: 471 us; the launch traced here: 475 us
  Pallas kernels  157 us (33%)
  waiting for transfers between devices  110 us (23%)
  between operations  69.8 us (15%)
  local copies, waits for them, and re-layouts  43.2 us (9%)
  starting transfers between devices  41.4 us (9%)
  blocking collectives  31.9 us (7%)
  other arithmetic  13.5 us (3%)
  matrix products  8.4 us (2%)
    pallas_call x1, Pallas kernels, pair_blocks(): pl.pallas_call(pair_kernel, out_shape=jax.ShapeDtypeStruct((members, sour...  127 us
    ppermute x10, waiting for transfers between devices, from_owner(): arrived = lax.ppermute(value, axis, steps)  62.3 us
    all_to_all x1, waiting for transfers between devices, local(): lax.all_to_all(send_basis, 'row', split_axis=0, concat_axis=1, tiled=True)  38.3 us
    all_gather x1, blocking collectives, local(): lax.all_gather(offsets, 'col', axis=1, tiled=True)  31.9 us
    pallas_call x2, Pallas kernels, factor_panel(): pl.pallas_call(panel_kernel, out_shape=[shape] * 3, in_specs=[spec], out_...  29.3 us
    unnamed x20, local copies, waits for them, and re-layouts  20.4 us
    all_to_all x1, starting transfers between devices, local(): lax.all_to_all(outgoing, 'row', split_axis=0, concat_axis=0, tiled=True)  13.7 us
    ppermute x10, starting transfers between devices, from_owner(): arrived = lax.ppermute(value, axis, steps)  13 us
  transfers between devices with their start and end apart: 20, of which 9 were waited for; matrix products, arithmetic and copies ran while one was open for 10% of the time, Pallas kernels for 0%

profile of v2, /device:TPU:0, one launch (start us, length us, event | category | flops | bytes accessed | tf_op | source)
XLA Modules:
  0.0 475.0 jit_solution(13268928261167366585)
XLA Ops:
  7.8 2.6 collective-permute-start.4
  46.2 31.9 %all_gather.6 = bf16[2,8,3,384]{3,0,2,1:T(2,128)(2,1)S(1)} all-gather(bf16[2,1,3,384]{3,0,2,1:T(2,128)(2,1)} %param.7), channel_id=1, replica_groups=mesh['row'=4,'col'=8] {'col'}, dimensions={1}, use_global_device_ids=true | all-gather | bytes 41472 | tf_op jit(solution)/shard_map/all_gather | solution.py:200
  89.1 3.3 all-to-all-start
  106.4 2.6 pad_add_fusion.1.row_counts
  110.6 2.0 constant_dynamic-update-slice_fusion.3
  116.9 1.9 dynamic-slice_dynamic-update-slice_fusion.15
  136.8 4.9 %all-to-all-start.1 = ((bf16[16,384,384]{2,1,0:T(8,128)(2,1)}), bf16[16,384,384]{2,1,0:T(8,128)(2,1)}, u32[]{:S(2)}, u32[]{:S(2)}) async-start(bf16[16,384,384]{2,1,0:T(8,128)(2,1)} %dynamic-slice_dynamic-update-slice_fusion), calls=%async_computation.1 | async-start | bytes 9437184 | tf_op jit(solution)/shard_map/all_to_all | solution.py:230
  149.9 2.3 copy.106
  152.3 2.1 bitcast_add_fusion.row_points_ref
  154.4 3.0 bitcast_select_fusion.1.basis_ref
  157.3 38.3 %all-to-all-done.1 = bf16[16,384,384]{2,1,0:T(8,128)(2,1)} async-done(((bf16[16,384,384]{2,1,0:T(8,128)(2,1)}), bf16[16,384,384]{2,1,0:T(8,128)(2,1)}, u32[]{:S(2)}, u32[]{:S(2)}) %all-to-all-start.1) | async-done | bytes 4718624 | tf_op jit(solution)/shard_map/all_to_all | solution.py:230
  195.6 2.9 copy.116
  200.2 127.4 %shard_map.64 = f32[4,2,128,128]{3,2,1,0:T(8,128)S(1)} custom-call(s32[4]{0:T(128)S(1)} %pad_add_fusion.1.row_counts, s32[2]{0:T(128)S(1)} %fusion.87.col_counts, f32[4,1536,3]{2,1,0:T(8,128)S(1)} %bitcast_add_fusion.row_points_ref, f32[2,3,1536]{2,1,0:T(4,128)S(1)} %convert_add_fusion.col_points_ref, bf16[4,1536,384]{2,1,0:T(8,128)(2,1)S(1)} %bitcast_select_fusion.test_ref, ...), custom_call_target="tpu_custom_call" | custom-call | tf_op jit(solution)/shard_map/pallas_call | solution.py:90
  328.6 13.7 %all-to-all-start.2 = ((f32[4,1,128,2,128]{4,2,3,1,0:T(8,128)}), f32[4,1,128,2,128]{4,2,3,1,0:T(8,128)S(1)}, u32[]{:S(2)}, u32[]{:S(2)}) async-start(f32[4,1,128,2,128]{4,2,3,1,0:T(8,128)} %maximum_select_fusion), calls=%async_computation.2 | async-start | bytes 1048576 | tf_op jit(solution)/shard_map/all_to_all | solution.py:253
  342.7 8.8 %all-to-all-done.2 = f32[4,1,128,2,128]{4,2,3,1,0:T(8,128)S(1)} async-done(((f32[4,1,128,2,128]{4,2,3,1,0:T(8,128)}), f32[4,1,128,2,128]{4,2,3,1,0:T(8,128)S(1)}, u32[]{:S(2)}, u32[]{:S(2)}) %all-to-all-start.2) | async-done | bytes 524320 | tf_op jit(solution)/shard_map/all_to_all | solution.py:253
  354.4 3.0 collective-permute-start.6
  357.5 5.7 %collective-permute-done.6 = f32[512,128]{1,0:T(8,128)S(1)} collective-permute-done((f32[512,128]{1,0:T(8,128)S(1)}, f32[512,128]{1,0:T(8,128)S(1)}, u32[]{:S(2)}, u32[]{:S(2)}) %collective-permute-start.6) | collective-permute-done | bytes 262176 | tf_op jit(solution)/shard_map/ppermute | solution.py:124
  364.5 5.0 %collective-permute-done.7 = f32[512,128]{1,0:T(8,128)S(1)} collective-permute-done((f32[512,128]{1,0:T(8,128)S(1)}, f32[512,128]{1,0:T(8,128)S(1)}, u32[]{:S(2)}, u32[]{:S(2)}) %collective-permute-start.7) | collective-permute-done | bytes 262176 | tf_op jit(solution)/shard_map/ppermute | solution.py:124
  371.3 4.1 collective-permute-done.8
  379.7 4.7 collective-permute-done.10
  384.4 14.6 %shard_map.65 = (f32[128,128]{1,0:T(8,128)S(1)}, f32[128,128]{1,0:T(8,128)S(1)}, f32[128,128]{1,0:T(8,128)S(1)}) custom-call(f32[128,128]{1,0:T(8,128)S(1)} %slice.204.block_ref), custom_call_target="tpu_custom_call" | custom-call | tf_op jit(solution)/shard_map/pallas_call | solution.py:167
  405.3 29.5 %collective-permute-done.13 = f32[512,128]{1,0:T(8,128)S(1)} collective-permute-done((f32[512,128]{1,0:T(8,128)S(1)}, f32[512,128]{1,0:T(8,128)S(1)}, u32[]{:S(2)}, u32[]{:S(2)}) %collective-permute-start.13) | collective-permute-done | bytes 262176 | tf_op jit(solution)/shard_map/ppermute | solution.py:124
  437.2 12.4 %collective-permute-done.15 = f32[128,384]{1,0:T(8,128)S(1)} collective-permute-done((f32[128,384]{1,0:T(8,128)S(1)}, f32[128,384]{1,0:T(8,128)S(1)}, u32[]{:S(2)}, u32[]{:S(2)}) %collective-permute-start.15) | collective-permute-done | bytes 196640 | tf_op jit(solution)/shard_map/ppermute | solution.py:124
  449.6 14.6 %shard_map.66 = (f32[128,128]{1,0:T(8,128)S(1)}, f32[128,128]{1,0:T(8,128)S(1)}, f32[128,128]{1,0:T(8,128)S(1)}) custom-call(f32[128,128]{1,0:T(8,128)S(1)} %slice.206.block_ref), custom_call_target="tpu_custom_call" | custom-call | tf_op jit(solution)/shard_map/pallas_call | solution.py:167
  (140 shorter events, 64.0 us)
Async XLA Ops:
  6.5 110.4 %all-gather.2.cloned.1.call-start = ((), (), s32[]{:S(2)}) async-start(), calls=%async_computation.3 | async-start | bytes 5308416 | tf_op jit(solution)/shard_map/all_gather | solution.py:199
  7.3 105.3 %collective-permute-start.3 = (bf16[2,1,384,384]{3,2,0,1:T(8,128)(2,1)}, bf16[2,1,384,384]{3,2,0,1:T(8,128)(2,1)S(1)}, u32[]{:S(2)}, u32[]{:S(2)}) collective-permute-start(bf16[2,1,384,384]{3,2,0,1:T(8,128)(2,1)} %bitcast.213), channel_id=1, source_target_pairs={{0,8},{8,16},{16,24},{24,0},{1,9},{9,17},{17,25},{25,1},{2,10},{10... | collective-permute-start | bytes 1769480 | tf_op jit(solution)/shard_map/ppermute | solution.py:106
  7.8 107.3 %collective-permute-start.4 = (bf16[2,1,384,384]{3,2,0,1:T(8,128)(2,1)}, bf16[2,1,384,384]{3,2,0,1:T(8,128)(2,1)S(1)}, u32[]{:S(2)}, u32[]{:S(2)}) collective-permute-start(bf16[2,1,384,384]{3,2,0,1:T(8,128)(2,1)} %bitcast.214), channel_id=1, source_target_pairs={{0,16},{8,24},{16,0},{24,8},{1,17},{9,25},{17,1},{25,9},{2,18},{10... | collective-permute-start | bytes 1769480 | tf_op jit(solution)/shard_map/ppermute | solution.py:106
  10.3 105.7 %collective-permute-start.5 = (bf16[2,1,384,384]{3,2,0,1:T(8,128)(2,1)}, bf16[2,1,384,384]{3,2,0,1:T(8,128)(2,1)S(1)}, u32[]{:S(2)}, u32[]{:S(2)}) collective-permute-start(bf16[2,1,384,384]{3,2,0,1:T(8,128)(2,1)} %bitcast.215), channel_id=1, source_target_pairs={{0,24},{8,0},{16,8},{24,16},{1,25},{9,1},{17,9},{25,17},{2,26},{10... | collective-permute-start | bytes 1769480 | tf_op jit(solution)/shard_map/ppermute | solution.py:106
  12.4 137.3 %collective-permute-start = (bf16[2,1,3,384]{3,2,0,1:T(4,128)(2,1)S(1)}, bf16[2,1,3,384]{3,2,0,1:T(4,128)(2,1)S(1)}, u32[]{:S(2)}, u32[]{:S(2)}) collective-permute-start(bf16[2,1,3,384]{3,2,0,1:T(4,128)(2,1)S(1)} %copy.108), channel_id=1, source_target_pairs={{0,8},{8,16},{16,24},{24,0},{1,9},{9,17},{17,25},{25,1},{2,10},{10... | collective-permute-start | bytes 13832 | tf_op jit(solution)/shard_map/ppermute | solution.py:106
  12.4 137.4 %collective-permute-start.1 = (bf16[2,1,3,384]{3,2,0,1:T(4,128)(2,1)S(1)}, bf16[2,1,3,384]{3,2,0,1:T(4,128)(2,1)S(1)}, u32[]{:S(2)}, u32[]{:S(2)}) collective-permute-start(bf16[2,1,3,384]{3,2,0,1:T(4,128)(2,1)S(1)} %copy.108), channel_id=1, source_target_pairs={{0,16},{8,24},{16,0},{24,8},{1,17},{9,25},{17,1},{25,9},{2,18},{10... | collective-permute-start | bytes 13832 | tf_op jit(solution)/shard_map/ppermute | solution.py:106
  89.1 47.7 %all-to-all-start = ((bf16[16,384,3]{1,2,0:T(4,128)(2,1)}), bf16[16,384,3]{1,2,0:T(4,128)(2,1)S(1)}, u32[]{:S(2)}, u32[]{:S(2)}) async-start(bf16[16,384,3]{1,2,0:T(4,128)(2,1)} %copy.104), calls=%async_computation | async-start | bytes 98304 | tf_op jit(solution)/shard_map/all_to_all | solution.py:231
  112.6 37.2 %collective-permute-start.2 = (bf16[2,1,3,384]{3,2,0,1:T(4,128)(2,1)S(1)}, bf16[2,1,3,384]{3,2,0,1:T(4,128)(2,1)S(1)}, u32[]{:S(2)}, u32[]{:S(2)}) collective-permute-start(bf16[2,1,3,384]{3,2,0,1:T(4,128)(2,1)S(1)} %copy.108), channel_id=1, source_target_pairs={{0,24},{8,0},{16,8},{24,16},{1,25},{9,1},{17,9},{25,17},{2,26},{10... | collective-permute-start | bytes 13832 | tf_op jit(solution)/shard_map/ppermute | solution.py:106
  116.9 13.9 %copy-start.1 = (bf16[2,8,384,384]{3,2,1,0:T(8,128)(2,1)S(1)}, bf16[2,8,384,384]{3,2,1,0:T(8,128)(2,1)}, u32[]{:S(2)}) copy-start(bf16[2,8,384,384]{3,2,1,0:T(8,128)(2,1)} %all-gather.2.cloned.1.call-done) | copy-start | bytes 14155780
  136.8 58.8 %all-to-all-start.1 = ((bf16[16,384,384]{2,1,0:T(8,128)(2,1)}), bf16[16,384,384]{2,1,0:T(8,128)(2,1)}, u32[]{:S(2)}, u32[]{:S(2)}) async-start(bf16[16,384,384]{2,1,0:T(8,128)(2,1)} %dynamic-slice_dynamic-update-slice_fusion), calls=%async_computation.1 | async-start | bytes 9437184 | tf_op jit(solution)/shard_map/all_to_all | solution.py:230
  198.6 1.7 copy-start
  328.6 22.9 %all-to-all-start.2 = ((f32[4,1,128,2,128]{4,2,3,1,0:T(8,128)}), f32[4,1,128,2,128]{4,2,3,1,0:T(8,128)S(1)}, u32[]{:S(2)}, u32[]{:S(2)}) async-start(f32[4,1,128,2,128]{4,2,3,1,0:T(8,128)} %maximum_select_fusion), calls=%async_computation.2 | async-start | bytes 1048576 | tf_op jit(solution)/shard_map/all_to_all | solution.py:253
  354.4 8.7 %collective-permute-start.6 = (f32[512,128]{1,0:T(8,128)S(1)}, f32[512,128]{1,0:T(8,128)S(1)}, u32[]{:S(2)}, u32[]{:S(2)}) collective-permute-start(f32[512,128]{1,0:T(8,128)S(1)} %fusion.6), channel_id=1, source_target_pairs={{0,1},{8,9},{16,17},{24,25}} | collective-permute-start | bytes 786440 | tf_op jit(solution)/shard_map/ppermute | solution.py:124
  363.1 6.4 %collective-permute-start.7 = (f32[512,128]{1,0:T(8,128)S(1)}, f32[512,128]{1,0:T(8,128)S(1)}, u32[]{:S(2)}, u32[]{:S(2)}) collective-permute-start(f32[512,128]{1,0:T(8,128)S(1)} %broadcast_select_fusion), channel_id=1, source_target_pairs={{0,2},{1,3},{8,10},{9,11},{16,18},{17,19},{24,26},{25,27}} | collective-permute-start | bytes 786440 | tf_op jit(solution)/shard_map/ppermute | solution.py:124
  369.6 5.8 %collective-permute-start.8 = (f32[512,128]{1,0:T(8,128)S(1)}, f32[512,128]{1,0:T(8,128)S(1)}, u32[]{:S(2)}, u32[]{:S(2)}) collective-permute-start(f32[512,128]{1,0:T(8,128)S(1)} %broadcast_select_fusion.1), channel_id=1, source_target_pairs={{0,4},{1,5},{2,6},{3,7},{8,12},{9,13},{10,14},{11,15},{16,20},{17,... | collective-permute-start | bytes 786440 | tf_op jit(solution)/shard_map/ppermute | solution.py:124
  375.7 2.4 collective-permute-start.9
  378.1 6.3 %collective-permute-start.10 = (f32[128,384]{1,0:T(8,128)S(1)}, f32[128,384]{1,0:T(8,128)S(1)}, u32[]{:S(2)}, u32[]{:S(2)}) collective-permute-start(f32[128,384]{1,0:T(8,128)S(1)} %broadcast_select_fusion.6), channel_id=1, source_target_pairs={{0,16},{8,24},{1,17},{9,25},{2,18},{10,26},{3,19},{11,27},{4,20},{... | collective-permute-start | bytes 589832 | tf_op jit(solution)/shard_map/ppermute | solution.py:124
  402.1 0.7 collective-permute-start.11
  402.9 0.7 collective-permute-start.12
  403.6 31.2 %collective-permute-start.13 = (f32[512,128]{1,0:T(8,128)S(1)}, f32[512,128]{1,0:T(8,128)S(1)}, u32[]{:S(2)}, u32[]{:S(2)}) collective-permute-start(f32[512,128]{1,0:T(8,128)S(1)} %broadcast_select_fusion.4), channel_id=1, source_target_pairs={{1,5},{2,6},{3,7},{4,0},{9,13},{10,14},{11,15},{12,8},{17,21},{18,... | collective-permute-start | bytes 786440 | tf_op jit(solution)/shard_map/ppermute | solution.py:124
  435.2 0.7 collective-permute-start.14
  435.9 13.7 %collective-permute-start.15 = (f32[128,384]{1,0:T(8,128)S(1)}, f32[128,384]{1,0:T(8,128)S(1)}, u32[]{:S(2)}, u32[]{:S(2)}) collective-permute-start(f32[128,384]{1,0:T(8,128)S(1)} %broadcast_select_fusion.8), channel_id=1, source_target_pairs={{8,24},{16,0},{9,25},{17,1},{10,26},{18,2},{11,27},{19,3},{12,28},... | collective-permute-start | bytes 589832 | tf_op jit(solution)/shard_map/ppermute | solution.py:124
Sparse Core Ops, SparseCore 0:
  9.5 83.2 all-gather.1
